TPU v7x, 512 devices: a whole 4x8x8 slice. The times are simulated.
512 devices in a mesh: blk: 16 (over y, core), pair: 16 (over z, x_hi), seq: 2 (over x_lo).
Axes of the slice: x: 4 (x_hi: 2, x_lo: 2; x = x_hi * 2 + x_lo), y: 8, z: 8, core: 2. Of those that a mesh axis runs over, the one named last changes fastest.
Arguments:
- resp_x: bfloat16 [16, 16, 256, 5120], P('blk', 'pair', 'seq'), may hold values from -6 to 6
- queries: bfloat16 [16, 16, 256, 2560], P('blk', 'pair', 'seq'), may hold values from -5 to 5
- key_weight: bfloat16 [5120, 512], P('blk'), may hold values from -0.078125 to 0.078125
- value_weight: bfloat16 [5120, 512], P('blk'), may hold values from -0.078125 to 0.078125
- prompt_key: bfloat16 [16, 2048, 512], P('blk', ('pair', 'seq')), may hold values from -5 to 5
- cached_prompt_values: bfloat16 [16, 2048, 512], P('blk', ('pair', 'seq')), may hold values from -6 to 6
- lengths: int32 [16, 16], P('blk', 'pair'), may hold values from 1 to 256, as said below
- prompt_len: int32 [16], P('blk'), may hold values from 1024 to 2048, as said below
Outputs:
- context: bfloat16 [16, 16, 256, 2560], P('blk', 'pair', 'seq')
Inputs may be any that keep to these rules, and one draw needn't show every extreme that they name: `lengths`: every response has at least one live position; some response of the batch has all 256 positions live. `prompt_len`: at least half of each prompt's cached positions are live; some prompt has all 2048 live.
All inputs are finite; a program needn't handle non-finite values.
Results may differ from a plain program's by a relative error of at most 0.0085.
Values may be sent and summed in bfloat16 or wider, within the bound.
A program may use at most 128 MiB of HBM per device.

v0:
```python
import jax
import jax.numpy as jnp
from jax import lax
from jax.sharding import PartitionSpec as P

KEY_VALUE_HEADS = 4
HEAD_SIZE = 128


NEGATIVE_FILL = -1e30


def local(
    resp_x, queries, key_weight, value_weight, prompt_key, cached_prompt_values, lengths, prompt_len
):
    hidden = resp_x[0, 0]
    query_matrix = queries[0, 0]
    row_list = hidden.shape[0]
    width = key_weight.shape[1]
    head_group = queries.shape[3] // width

    def add_rows(piece):
        return jnp.dot(hidden, piece, preferred_element_type=jnp.float32)

    key_sum = add_rows(lax.all_gather(key_weight, "blk", axis=0, tiled=True))
    value_sum = add_rows(lax.all_gather(value_weight, "blk", axis=0, tiled=True))
    new_key = key_sum.astype(jnp.bfloat16)
    new_value = value_sum.astype(jnp.bfloat16)
    seq_rank = lax.axis_index("seq")
    query_pos = seq_rank * row_list + jnp.arange(row_list, dtype=jnp.int32)
    query_head_rows = query_matrix.reshape(row_list, KEY_VALUE_HEADS, head_group, HEAD_SIZE)
    scale = HEAD_SIZE ** (-0.5)

    def block_update(carry, key_matrix, value_matrix, allowed):
        top, denom, total_sum = carry
        count_total = key_matrix.shape[0]
        key_head_rows = key_matrix.reshape(count_total, KEY_VALUE_HEADS, HEAD_SIZE)
        value_head_rows = value_matrix.reshape(count_total, KEY_VALUE_HEADS, HEAD_SIZE)
        scores = (
            jnp.einsum(
                "rhgd,khd->hgrk", query_head_rows, key_head_rows, preferred_element_type=jnp.float32
            )
            * scale
        )
        scores = jnp.where(allowed, scores, NEGATIVE_FILL)
        new_top = jnp.maximum(top, jnp.max(scores, axis=-1))
        weight = jnp.where(allowed, jnp.exp(scores - new_top[..., None]), 0.0)
        fade = jnp.exp(top - new_top)
        denom = denom * fade + jnp.sum(weight, axis=-1)
        update = jnp.einsum(
            "hgrk,khd->hgrd",
            weight.astype(jnp.bfloat16),
            value_head_rows,
            preferred_element_type=jnp.float32,
        )
        total_sum = total_sum * fade[..., None] + update
        return (new_top, denom, total_sum)

    live_prompt = prompt_len[0]
    init = (
        jnp.full((KEY_VALUE_HEADS, head_group, row_list), NEGATIVE_FILL, jnp.float32),
        jnp.zeros((KEY_VALUE_HEADS, head_group, row_list), jnp.float32),
        jnp.zeros((KEY_VALUE_HEADS, head_group, row_list, HEAD_SIZE), jnp.float32),
    )
    pieces = (
        lax.all_gather(prompt_key[0], ("pair", "seq"), axis=0, tiled=True),
        lax.all_gather(cached_prompt_values[0], ("pair", "seq"), axis=0, tiled=True),
    )
    count_total = pieces[0].shape[0]
    key_pos = jnp.arange(count_total, dtype=jnp.int32)
    allowed = jnp.broadcast_to((key_pos < live_prompt)[None, :], (row_list, count_total))
    carry = block_update(init, pieces[0], pieces[1], allowed)
    stacked = jnp.stack([new_key, new_value])
    joined = lax.all_gather(stacked, "seq", axis=1, tiled=True)
    key_pos = jnp.arange(joined.shape[1], dtype=jnp.int32)
    allowed = key_pos[None, :] <= query_pos[:, None]
    carry = block_update(carry, joined[0], joined[1], allowed)
    top, denom, total_sum = carry
    mixed_rows = total_sum / denom[..., None]
    mixed_rows = jnp.transpose(mixed_rows, (2, 0, 1, 3)).reshape(
        row_list, KEY_VALUE_HEADS * head_group * HEAD_SIZE
    )
    live = (query_pos < lengths[0, 0])[:, None]
    return jnp.where(live, mixed_rows, 0.0).astype(jnp.bfloat16)[None, None]


def solution(mesh):
    return jax.shard_map(
        local,
        mesh=mesh,
        in_specs=(
            P("blk", "pair", "seq", None),
            P("blk", "pair", "seq", None),
            P("blk", None),
            P("blk", None),
            P("blk", ("pair", "seq"), None),
            P("blk", ("pair", "seq"), None),
            P("blk", "pair"),
            P("blk"),
        ),
        out_specs=P("blk", "pair", "seq", None),
        check_vma=False,
    )
```

profile of v0, /device:TPU:1, one launch (start us, length us, event | category | flops | bytes accessed | tf_op | source)
XLA Modules:
  0.0 320.6 jit_solution(13620430635210305946)
XLA Ops:
  6.5 0.7 all-gather.11.cloned.1.call-update
  7.3 0.7 all-gather.13.cloned.1.call-update
  8.1 0.7 all-gather.9.cloned.1.call-update
  8.8 0.5 all-gather.7.cloned.1.call-update
  9.3 2.2 copy.29
  12.9 83.2 %all-gather.11.cloned.1.call-done = bf16[1,2048,512]{2,1,0:T(8,128)(2,1)} async-done(((bf16[1,64,512]{2,1,0:T(8,128)(2,1)}), bf16[1,2048,512]{2,1,0:T(8,128)(2,1)}) %all-gather.11.cloned.1.call-update) | async-done | bytes 2097168 | tf_op jit(solution)/shard_map/all_gather | solution.py:66
  96.0 2.9 copy.28
  99.0 81.1 %all-gather.13.cloned.1.call-done = bf16[1,2048,512]{2,1,0:T(8,128)(2,1)} async-done(((bf16[1,64,512]{2,1,0:T(8,128)(2,1)}), bf16[1,2048,512]{2,1,0:T(8,128)(2,1)}) %all-gather.13.cloned.1.call-update) | async-done | bytes 2097168 | tf_op jit(solution)/shard_map/all_gather | solution.py:67
  180.1 4.0 %copy.32 = bf16[1,2048,512]{1,2,0:T(8,128)(2,1)} copy(bf16[1,2048,512]{2,1,0:T(8,128)(2,1)} %all-gather.13.cloned.1.call-done) | data formatting | bytes 4194304 | tf_op jit(solution)/shard_map/all_gather | solution.py:67
  184.0 10.4 %bitcast_reduce_fusion = (f32[4,5,128]{2,1,0:T(8,128)S(1)}, f32[4,2048,128,5]{2,1,3,0:T(8,128)}) fusion(pred[2048]{0:T(1024)(128)(4,1)S(1)} %iota_compare_fusion.1, bf16[2048,4,128,1]{0,2,3,1:T(8,128)(2,1)S(1)} %bitcast.108, bf16[128,4,5,128]{0,3,2,1:T(8,128)(2,1)} %bitcast.109), kind=kOutput, calls=%fused_computation.1 | convolution fusion | flops 1357903360 | bytes 23736320 | tf_op jit(solution)/shard_map/rhgd,khd->hgrk/dot_general | solution.py:40
  194.4 34.9 %all-gather.9.cloned.1.call-done = bf16[5120,512]{1,0:T(8,128)(2,1)} async-done(((bf16[320,512]{1,0:T(8,128)(2,1)}), bf16[5120,512]{1,0:T(8,128)(2,1)}) %all-gather.9.cloned.1.call-update) | async-done | bytes 5242896 | tf_op jit(solution)/shard_map/all_gather | solution.py:26
  229.3 3.3 %fusion.38 = bf16[1,128,512]{2,1,0:T(8,128)(2,1)S(1)} fusion(bf16[5120,512]{1,0:T(8,128)(2,1)} %all-gather.9.cloned.1.call-done, bf16[1,1,128,5120]{3,2,1,0:T(8,128)(2,1)S(1)} %copy-done), kind=kOutput, calls=%fused_computation.33 | convolution fusion | flops 671154176 | bytes 6684672 | tf_op jit(solution)/shard_map/dot_general | solution.py:23
  232.6 43.4 %all-gather.7.cloned.1.call-done = bf16[5120,512]{1,0:T(8,128)(2,1)} async-done(((bf16[320,512]{1,0:T(8,128)(2,1)}), bf16[5120,512]{1,0:T(8,128)(2,1)}) %all-gather.7.cloned.1.call-update) | async-done | bytes 5242896 | tf_op jit(solution)/shard_map/all_gather | solution.py:25
  276.1 3.3 %fusion.41 = bf16[1,128,512]{2,1,0:T(8,128)(2,1)S(1)} fusion(bf16[5120,512]{1,0:T(8,128)(2,1)} %all-gather.7.cloned.1.call-done, bf16[1,1,128,5120]{3,2,1,0:T(8,128)(2,1)S(1)} %copy-done), kind=kOutput, calls=%fused_computation.34 | convolution fusion | flops 671154176 | bytes 6684672 | tf_op jit(solution)/shard_map/dot_general | solution.py:23
  279.5 8.6 %all_gather.19 = bf16[2,256,512]{2,1,0:T(8,128)(2,1)S(1)} all-gather(bf16[2,128,512]{2,1,0:T(8,128)(2,1)S(1)} %pad_maximum_fusion), channel_id=1, replica_groups=mesh['blk'=16,'pair'=16,'seq'=2] {'seq'}, dimensions={1}, use_global_device_ids=true | all-gather | bytes 786432 | tf_op jit(solution)/shard_map/all_gather | solution.py:74
  288.2 0.1 copy.51
  288.4 0.5 fusion.8
  288.9 0.6 fusion.9
  289.6 11.1 %fusion.2 = f32[4,5,128]{2,1,0:T(8,128)S(1)} fusion(f32[4,2048,128,5]{2,1,3,0:T(8,128)} %get-tuple-element.15, f32[4,5,128]{2,1,0:T(8,128)S(1)} %get-tuple-element.11, pred[2048]{0:T(1024)(128)(4,1)S(1)} %iota_compare_fusion.1), kind=kLoop, calls=%fused_computation.5 | loop fusion | flops 26211840 | bytes 20994048 | tf_op jit(solution)/shard_map/reduce_sum | solution.py:49
  300.7 1.8 copy-done.1
  302.6 8.1 %fusion.19 = f32[128,4,5,128]{0,3,2,1:T(8,128)} fusion(bf16[2048,4,128,1]{0,2,3,1:T(8,128)(2,1)} %bitcast.111, f32[4,2048,128,5]{2,1,3,0:T(8,128)S(1)} %copy-done.1, f32[4,5,128]{2,1,0:T(8,128)S(1)} %get-tuple-element.11, pred[2048]{0:T(1024)(128)(4,1)S(1)} %iota_compare_fusion.1, f32[128,4,5]{0,2,1:T(8,128)S(1)} %get-tuple-element.6, ...), kind=kOutput, calls=%fused_computation.20 | convolution fusion | flops 1369047040 | bytes 24412160 | tf_op jit(solution)/shard_map/hgrk,khd->hgrd/dot_general | solution.py:50
  310.6 2.2 fusion.15
  312.8 0.2 copy.38
  313.1 1.0 select_convert_fusion
  (18 shorter events, 0.3 us)
Async XLA Ops:
  6.5 222.8 %copy-start = (bf16[1,1,128,5120]{3,2,1,0:T(8,128)(2,1)S(1)}, bf16[1,1,128,5120]{3,2,1,0:T(8,128)(2,1)}, u32[]{:S(2)}) copy-start(bf16[1,1,128,5120]{3,2,1,0:T(8,128)(2,1)} %param.8) | copy-start | bytes 3932164
  6.5 89.5 %all-gather.11.cloned.1.call-start = ((), (), s32[]{:S(2)}) async-start(), calls=%async_computation.2 | async-start | bytes 2162688 | tf_op jit(solution)/shard_map/all_gather | solution.py:66
  7.3 172.8 %all-gather.13.cloned.1.call-start = ((), (), s32[]{:S(2)}) async-start(), calls=%async_computation.3 | async-start | bytes 2162688 | tf_op jit(solution)/shard_map/all_gather | solution.py:67
  8.0 221.3 %all-gather.9.cloned.1.call-start = ((), (), s32[]{:S(2)}) async-start(), calls=%async_computation.1 | async-start | bytes 5570560 | tf_op jit(solution)/shard_map/all_gather | solution.py:26
  8.7 267.3 %all-gather.7.cloned.1.call-start = ((), (), s32[]{:S(2)}) async-start(), calls=%async_computation | async-start | bytes 5570560 | tf_op jit(solution)/shard_map/all_gather | solution.py:25
  279.4 8.9 %copy-start.2 = (bf16[1,1,128,2560]{2,3,1,0:T(8,128)(2,1)S(1)}, bf16[1,1,128,2560]{2,3,1,0:T(8,128)(2,1)}, u32[]{:S(2)}) copy-start(bf16[1,1,128,2560]{2,3,1,0:T(8,128)(2,1)} %copy.29) | copy-start | bytes 1966084
  289.6 13.0 %copy-start.1 = (f32[4,2048,128,5]{2,1,3,0:T(8,128)S(1)}, f32[4,2048,128,5]{2,1,3,0:T(8,128)}, u32[]{:S(2)}) copy-start(f32[4,2048,128,5]{2,1,3,0:T(8,128)} %get-tuple-element.15) | copy-start | bytes 62914564
Sparse Core Ops, SparseCore 0:
  10.5 85.4 all-gather.10
  99.2 80.8 all-gather.12
  182.2 47.0 all-gather.8
  231.3 44.7 all-gather.6
where the time goes:
time: 321 us
  waiting for transfers between devices  245 us (76%)
  matrix products  27.8 us (9%)
  between operations  14.6 us (5%)
  other arithmetic  12.9 us (4%)
  local copies, waits for them, and re-layouts  11.4 us (4%)
  blocking collectives  8.64 us (3%)
    all_gather x1, waiting for transfers between devices, local(): lax.all_gather(prompt_key[0], ('pair', 'seq'), axis=0, tiled=True)  83.2 us
    all_gather x1, waiting for transfers between devices, local(): lax.all_gather(cached_prompt_values[0], ('pair', 'seq'), axis=0, tiled=True)  81.1 us
    all_gather x1, waiting for transfers between devices, local(): key_sum = add_rows(lax.all_gather(key_weight, 'blk', axis=0, tiled=True))  43.4 us
    all_gather x1, waiting for transfers between devices, local(): lax.all_gather(value_weight, 'blk', axis=0, tiled=True)  34.9 us
    reduce_sum x2, other arithmetic, block_update(): denom = denom * fade + jnp.sum(weight, axis=-1)  11.8 us
    dot_general x2, matrix products, block_update(): jnp.einsum('rhgd,khd->hgrk', query_head_rows, key_head_rows, preferred_el...  10.9 us
    dot_general x2, matrix products, block_update(): jnp.einsum('hgrk,khd->hgrd', weight.astype(jnp.bfloat16), value_head_rows...  10.2 us
    all_gather x1, blocking collectives, local(): joined = lax.all_gather(stacked, 'seq', axis=1, tiled=True)  8.64 us
  transfers between devices with their start and end apart: 4, of which 4 were waited for; matrix products, arithmetic and copies ran while one was open for 7% of the time, Pallas kernels for 0%

commit v1 on v0

v1 whole, which is shorter than its diff:
```python
import functools
import math

import jax
import jax.numpy as jnp
from jax import lax
from jax.experimental import pallas as pl
from jax.experimental.pallas import tpu as pltpu
from jax.sharding import PartitionSpec as P

KV_HEADS = 4
HEAD = 128
GROUP = 5
NY, NZ, NX = 8, 8, 4
ROWS = 128
SHARD = 64
BLOCK = NX * SHARD
WROWS = 320
XCOLS = 2 * WROWS
GCOLS = 256
QROWS = GROUP * ROWS
NEG = -1e30
SCALE = HEAD ** (-0.5) * math.log2(math.e)
MESH = pl.DeviceIdType.MESH
F32 = jnp.float32
BF16 = jnp.bfloat16
U = 3.3
W = 4.0
ZS = 5.0


def kernel(
    x_ref, q_ref, kw_ref, vw_ref, pk_ref, pv_ref, plen_ref, o_ref,
    kvbuf, wbuf, xbuf, qs, pacc, psend, precv, newkv, top_ref, den_ref, acc_ref,
    own_sem, q_sem, xl_sem, wl_sem,
    ph_s, ph_r, zs_s, zs_r, h_s, h_r, y_s, y_r, b_s, b_r, x_s, x_r, p_s, p_r,
):
    blk, pair, s = lax.axis_index("blk"), lax.axis_index("pair"), lax.axis_index("seq")
    y, c = blk // 2, blk % 2
    z, hi = pair // 2, pair % 2
    x = hi * 2 + s
    q = (y + s) % 2

    def y_dev(step):
        return {"blk": ((y + step + NY) % NY) * 2 + c, "pair": pair, "seq": s}

    def z_dev(step):
        return {"blk": blk, "pair": ((z + step + NZ) % NZ) * 2 + hi, "seq": s}

    sib = {"blk": y * 2 + (1 - c), "pair": pair, "seq": s}
    sx = {"blk": blk, "pair": pair, "seq": 1 - s}
    hx = {"blk": blk, "pair": z * 2 + (1 - hi), "seq": 1 - s}
    x2 = {"blk": blk, "pair": z * 2 + (1 - hi), "seq": s}
    x_peers = (sx, hx, x2)
    peer_x = (hi * 2 + 1 - s, 3 - x, (1 - hi) * 2 + s)

    def remote(src, dst, ss, rs, dev):
        return pltpu.make_async_remote_copy(
            src_ref=src, dst_ref=dst, send_sem=ss, recv_sem=rs, device_id=dev, device_id_type=MESH
        )

    sends = []

    local_q = [
        pltpu.make_async_copy(
            q_ref.at[0, 0, :, pl.ds((h * GROUP + g) * HEAD, HEAD)],
            qs.at[h, pl.ds(g * ROWS, ROWS)],
            q_sem.at[h * GROUP + g],
        )
        for h in range(KV_HEADS)
        for g in range(GROUP)
    ]
    cached = (pk_ref, pv_ref)
    own_rows = pl.ds(pl.multiple_of(x * SHARD, SHARD), SHARD)
    local_kv = [
        pltpu.make_async_copy(cached[i].at[0], kvbuf.at[i, z, own_rows], own_sem.at[i]) for i in range(2)
    ]
    own_x_rows = pl.ds(pl.multiple_of(s * ROWS, ROWS), ROWS)

    def x_cols(t, parity):
        return pl.ds(pl.multiple_of((2 * t + parity) * XCOLS, HEAD), XCOLS)

    local_x = [
        pltpu.make_async_copy(x_ref.at[0, 0, :, x_cols(t, s)], xbuf.at[t, own_x_rows], xl_sem.at[t])
        for t in range(4)
    ]
    weights = (kw_ref, vw_ref)

    def own_w(g):
        return weights[g // 2].at[:, pl.ds((g % 2) * GCOLS, GCOLS)]

    w_rows = pl.ds(pl.multiple_of(c * WROWS, 64), WROWS)
    w_other = pl.ds(pl.multiple_of((1 - c) * WROWS, 64), WROWS)
    local_w = [
        pltpu.make_async_copy(own_w(g), wbuf.at[g, y // 2, w_rows], wl_sem.at[g]) for g in range(4)
    ]
    for copy in local_kv + local_q + local_x:
        copy.start()

    @pl.when(q == 0)
    def _():
        for copy in local_w:
            copy.start()

    barrier = pltpu.get_barrier_semaphore()
    for dev in (sib, sx, hx, x2, y_dev(1), y_dev(-1), z_dev(1), z_dev(-1)):
        pl.semaphore_signal(barrier, inc=1, device_id=dev, device_id_type=MESH)
    pl.semaphore_wait(barrier, 8)

    phase = []
    for p in (2, 0, 1):
        for i in range(2):
            copy = remote(cached[i].at[0], kvbuf.at[i, z, own_rows], ph_s.at[i, p], ph_r.at[i, p], x_peers[p])
            copy.start()
            phase.append((i, p, copy))

    REACH = {(0, 0): 4, (0, 1): 3, (1, 0): 3, (1, 1): 4}

    def reach(way, g):
        return REACH[(way, g % 2)]

    def y_step(way):
        return 1 if way == 0 else -1

    def y_from(way, d):
        return (y - d + NY) % NY if way == 0 else (y + d) % NY

    def y_send(way, g, d, src):
        t = y_from(way, d) // 2
        return remote(
            src, wbuf.at[g, t, w_rows], y_s.at[way, g, d], y_r.at[way, g, d + 1], y_dev(y_step(way))
        )

    def y_recv(way, g, d):
        t = y_from(way, d) // 2
        ref = wbuf.at[g, t, w_rows]
        return remote(ref, ref, y_s.at[way, g, d], y_r.at[way, g, d], y_dev(-y_step(way)))

    def sib_send(g, t, src):
        return remote(src, wbuf.at[g, t, w_rows], b_s.at[g, t], b_r.at[g, t], sib)

    def sib_recv(g, t):
        ref = wbuf.at[g, t, w_other]
        return remote(ref, ref, b_s.at[g, t], b_r.at[g, t], sib)

    @pl.when(q == 0)
    def _():
        for g in range(4):
            for way in range(2):
                y_send(way, g, 0, own_w(g)).start()
            sib_send(g, y // 2, own_w(g)).start()

    def y_event(way, g, k, role):
        d = 2 * k - role
        if d > reach(way, g):
            return

        @pl.when(q == role)
        def _():
            y_recv(way, g, d).wait_recv()
            t = y_from(way, d) // 2
            if d < reach(way, g):
                y_send(way, g, d, wbuf.at[g, t, w_rows]).start()
            sib_send(g, t, wbuf.at[g, t, w_rows]).start()

    ring_cols = pl.ds(pl.multiple_of(s * HEAD, HEAD), 3 * HEAD)
    give_cols = pl.ds(pl.multiple_of(s * 3 * HEAD, HEAD), HEAD)
    take_cols = pl.ds(pl.multiple_of((1 - s) * 3 * HEAD, HEAD), HEAD)

    def z_from(way, d):
        return (z - d + NZ) % NZ if way == 0 else (z + d) % NZ

    def z_reach(way, i):
        return REACH[(way, i)]

    def z_send(way, i, d):
        ref = kvbuf.at[i, z_from(way, d), :, ring_cols]
        return remote(ref, ref, zs_s.at[way, i, d], zs_r.at[way, i, d + 1], z_dev(1 if way == 0 else -1))

    def z_recv(way, i, d):
        ref = kvbuf.at[i, z_from(way, d), :, ring_cols]
        return remote(ref, ref, zs_s.at[way, i, d], zs_r.at[way, i, d], z_dev(-1 if way == 0 else 1))

    def h_send(way, i, d):
        ref = kvbuf.at[i, z_from(way, d), :, give_cols]
        return remote(ref, ref, h_s.at[way, i, d], h_r.at[way, i, d], hx)

    def h_recv(way, i, d):
        ref = kvbuf.at[i, z_from(way, d), :, take_cols]
        return remote(ref, ref, h_s.at[way, i, d], h_r.at[way, i, d], hx)

    def z_event(way, i, d):
        z_recv(way, i, d).wait_recv()
        if d < z_reach(way, i):
            copy = z_send(way, i, d)
            copy.start()
            sends.append(copy)
        copy = h_send(way, i, d)
        copy.start()
        sends.append(copy)

    x_sends = [
        remote(x_ref.at[0, 0, :, x_cols(t, 1 - s)], xbuf.at[t, own_x_rows], x_s.at[t], x_r.at[t], sx)
        for t in range(4)
    ]
    other_x_rows = pl.ds(pl.multiple_of((1 - s) * ROWS, ROWS), ROWS)

    def start_z():
        for i, p, copy in phase:
            rows = pl.ds(pl.multiple_of(peer_x[p] * SHARD, SHARD), SHARD)
            ref = kvbuf.at[i, z, rows]
            remote(ref, ref, ph_s.at[i, p], ph_r.at[i, p], x_peers[p]).wait_recv()
        for copy in local_kv:
            copy.wait()
        for i in range(2):
            for way in range(2):
                copy = z_send(way, i, 0)
                copy.start()
                sends.append(copy)
        for copy in x_sends:
            copy.start()
            sends.append(copy)

    live_prompt = plen_ref[0]

    def update(h, score, value, first):
        best = functools.reduce(jnp.maximum, [jnp.max(v, axis=1, keepdims=True) for v in score])
        if first:
            top = jnp.broadcast_to(best, (QROWS, HEAD))
        else:
            old = top_ref[h]
            top = jnp.maximum(old, best)
            fade = jnp.exp2(old - top)
        weight = [jnp.exp2(v - top[:, :1]) for v in score]
        den = functools.reduce(
            jnp.add,
            [w[:, j * HEAD : (j + 1) * HEAD] for w in weight for j in range(w.shape[1] // HEAD)],
        )
        out = functools.reduce(
            jnp.add,
            [jnp.dot(w.astype(BF16), v, preferred_element_type=F32) for w, v in zip(weight, value)],
        )
        if not first:
            den = den + den_ref[h] * fade
            out = out + acc_ref[h] * fade
        return top, den, out

    def dot_t(a, b):
        return lax.dot_general(a, b, (((1,), (1,)), ((), ())), preferred_element_type=F32)

    def attend(blocks, first=False):
        def one(h, carry):
            cols = pl.ds(pl.multiple_of(h * HEAD, HEAD), HEAD)
            query = qs[h]
            score, value = [], []
            for zb in blocks:
                key = kvbuf[0, zb, :, cols]
                pos = zb * BLOCK + lax.broadcasted_iota(jnp.int32, (1, BLOCK), 1)
                shut = jnp.where(pos < live_prompt, 0.0, NEG)
                score.append(dot_t(query, key) * SCALE + shut)
                value.append(kvbuf[1, zb, :, cols])
            top, den, out = update(h, score, value, first)
            top_ref[h] = top
            den_ref[h] = den
            acc_ref[h] = out
            return carry

        lax.fori_loop(0, KV_HEADS, one, 0)

    def attend_distance(d):
        blocks = []
        if d < 4:
            for way in range(2):
                for i in range(2):
                    h_recv(way, i, d).wait_recv()
                blocks.append(z_from(way, d))
        else:
            h_recv(0, 0, 4).wait_recv()
            h_recv(1, 1, 4).wait_recv()
            blocks.append(z_from(0, 4))
        attend(blocks)

    order = ((y - q + NY) % NY, (y - 2 + 3 * q + NY) % NY, (y + 2 - 5 * q + NY) % NY, (y + 4 - q) % NY)

    def project(g, n):
        t = order[n] // 2
        sib_recv(g, t).wait_recv()
        if n == 0:

            @pl.when(q == 0)
            def _():
                local_w[g].wait()

        add = jnp.dot(xbuf[t], wbuf[g, t], preferred_element_type=F32)
        cols = pl.ds(g * GCOLS, GCOLS)
        if n == 0:
            pacc[:, cols] = add
        elif n < 3:
            pacc[:, cols] += add
        else:
            total = pacc[:, cols] + add
            pacc[:, cols] = total
            psend[g] = total.astype(BF16)
            copy = remote(psend.at[g], precv.at[g], p_s.at[g], p_r.at[g], sx)
            copy.start()
            sends.append(copy)

    def wait_x():
        for t in range(4):
            local_x[t].wait()
            ref = xbuf.at[t, other_x_rows]
            remote(ref, ref, x_s.at[t], x_r.at[t], sx).wait_recv()

    def join(g):
        remote(psend.at[g], precv.at[g], p_s.at[g], p_r.at[g], sx).wait_recv()
        newkv[g] = (pacc[:, g * GCOLS : (g + 1) * GCOLS] + precv[g].astype(F32)).astype(BF16)

    def attend_own():
        for copy in local_q:
            copy.wait()
        attend([z], first=True)

    def finish():
        row = lax.broadcasted_iota(jnp.int32, (QROWS, 2 * ROWS), 0) % ROWS + s * ROWS
        col = lax.broadcasted_iota(jnp.int32, (QROWS, 2 * ROWS), 1)
        shut = jnp.where(col <= row, 0.0, NEG)
        for h in range(KV_HEADS):
            cols = slice((h % 2) * HEAD, (h % 2 + 1) * HEAD)
            score = dot_t(qs[h], newkv[h // 2, :, cols]) * SCALE + shut
            _, den, out = update(h, [score], [newkv[2 + h // 2, :, cols]], False)
            out = out / jnp.sum(den, axis=1, keepdims=True)
            for g in range(GROUP):
                o_ref[:, (h * GROUP + g) * HEAD : (h * GROUP + g + 1) * HEAD] = out[
                    g * ROWS : (g + 1) * ROWS
                ].astype(BF16)

    plan = []

    def at(time, fn, *args):
        plan.append((time, len(plan), fn, args))

    at(0.0, start_z)
    at(ZS + 0.2, attend_own)
    for d in range(1, 5):
        for i in range(2):
            for way in range(2):
                if d <= z_reach(way, i):
                    at(ZS + min(2 * d - 1 + i, 7) * W, z_event, way, i, d)
        at(ZS + min(2 * d, 7) * W + 3.0, attend_distance, d)
    for role in range(2):
        for g in range(4):
            for k in (1, 2):
                for way in range(2):
                    at((g + 4 * k - 2 - role) * U, y_event, way, g, k, role)
    at(18.0, wait_x)
    for g in range(4):
        at(18.1 + g * 0.5, project, g, 0)
        at(18.2 + g * 0.5, project, g, 1)
        at((g + 6) * U + 2.0, project, g, 2)
        at((g + 6) * U + 2.1, project, g, 3)
        at((g + 6) * U + 7.0, join, g)
    for _, _, fn, args in sorted(plan, key=lambda e: e[:2]):
        fn(*args)
    finish()

    for copy in sends:
        copy.wait_send()
    for _, _, copy in phase:
        copy.wait_send()
    for role in range(2):

        @pl.when(q == role)
        def _():
            for g in range(4):
                for way in range(2):
                    if role == 0:
                        y_send(way, g, 0, own_w(g)).wait_send()
                    for k in (1, 2):
                        d = 2 * k - role
                        if d < reach(way, g):
                            y_send(way, g, d, wbuf.at[g, 0, w_rows]).wait_send()

    for g in range(4):
        for t in range(4):
            sib_send(g, t, wbuf.at[g, t, w_rows]).wait_send()


def attention(resp_x, queries, key_weight, value_weight, prompt_key, prompt_values, prompt_len):
    dma = pltpu.SemaphoreType.DMA
    any_space = pl.BlockSpec(memory_space=pl.ANY)
    return pl.pallas_call(
        kernel,
        out_shape=jax.ShapeDtypeStruct((ROWS, KV_HEADS * GROUP * HEAD), BF16),
        in_specs=[any_space] * 6 + [pl.BlockSpec(memory_space=pltpu.SMEM)],
        out_specs=pl.BlockSpec(memory_space=pltpu.VMEM),
        scratch_shapes=[
            pltpu.VMEM((2, NZ, BLOCK, KV_HEADS * HEAD), BF16),
            pltpu.VMEM((4, 4, XCOLS, GCOLS), BF16),
            pltpu.VMEM((4, 2 * ROWS, XCOLS), BF16),
            pltpu.VMEM((KV_HEADS, QROWS, HEAD), BF16),
            pltpu.VMEM((2 * ROWS, 4 * GCOLS), F32),
            pltpu.VMEM((4, 2 * ROWS, GCOLS), BF16),
            pltpu.VMEM((4, 2 * ROWS, GCOLS), BF16),
            pltpu.VMEM((4, 2 * ROWS, GCOLS), BF16),
            pltpu.VMEM((KV_HEADS, QROWS, HEAD), F32),
            pltpu.VMEM((KV_HEADS, QROWS, HEAD), F32),
            pltpu.VMEM((KV_HEADS, QROWS, HEAD), F32),
            dma((2,)), dma((KV_HEADS * GROUP,)), dma((4,)), dma((4,)),
            dma((2, 3)), dma((2, 3)),
            dma((2, 2, 5)), dma((2, 2, 5)),
            dma((2, 2, 5)), dma((2, 2, 5)),
            dma((2, 4, 5)), dma((2, 4, 5)),
            dma((4, 4)), dma((4, 4)),
            dma((4,)), dma((4,)),
            dma((4,)), dma((4,)),
        ],
        compiler_params=pltpu.CompilerParams(
            collective_id=0, has_side_effects=True, vmem_limit_bytes=56 << 20
        ),
        cost_estimate=pl.CostEstimate(flops=4_400_000_000, bytes_accessed=8_000_000, transcendentals=6_000_000),
    )(resp_x, queries, key_weight, value_weight, prompt_key, prompt_values, prompt_len)


def local(
    resp_x, queries, key_weight, value_weight, prompt_key, cached_prompt_values, lengths, prompt_len
):
    mixed = attention(
        resp_x, queries, key_weight, value_weight, prompt_key, cached_prompt_values, prompt_len
    )
    row = lax.axis_index("seq") * ROWS + jnp.arange(ROWS, dtype=jnp.int32)
    live = (row < lengths[0, 0])[:, None]
    return jnp.where(live, mixed, jnp.zeros((), BF16))[None, None]


def solution(mesh):
    return jax.shard_map(
        local,
        mesh=mesh,
        in_specs=(
            P("blk", "pair", "seq", None),
            P("blk", "pair", "seq", None),
            P("blk", None),
            P("blk", None),
            P("blk", ("pair", "seq"), None),
            P("blk", ("pair", "seq"), None),
            P("blk", "pair"),
            P("blk"),
        ),
        out_specs=P("blk", "pair", "seq", None),
        check_vma=False,
    )
```

time: 321 us -> 81.2 us (0.25)
  waiting for transfers between devices: 245 us -> 0 us
  Pallas kernels: 0 us -> 77.7 us
  matrix products: 27.8 us -> 0 us
  between operations: 14.6 us -> 1.31 us
  local copies, waits for them, and re-layouts: 11.4 us -> 0 us
  other arithmetic: 12.9 us -> 2.05 us
  blocking collectives: 8.64 us -> 0 us
    all_gather x4 -> x0, waiting for transfers between devices: 243 us -> none  [the longest x1 83.2 us: local(): lax.all_gather(prompt_key[0], ('pair', 'seq'), axis=0, tiled=True)]
    pallas_call x0 -> x1, Pallas kernels: none -> 77.7 us  [attention(): pl.pallas_call(kernel, out_shape=jax.ShapeDtypeStruct((ROWS, KV_HEADS * G...]
    dot_general x6 -> x0, matrix products: 27.8 us -> none  [the longest x2 10.9 us: block_update(): jnp.einsum('rhgd,khd->hgrk', query_head_rows, key_head_rows, preferred_el...]
    reduce_sum x2 -> x0, other arithmetic: 11.8 us -> none  [block_update(): denom = denom * fade + jnp.sum(weight, axis=-1)]
    all_gather x1 -> x0, blocking collectives: 8.64 us -> none  [local(): joined = lax.all_gather(stacked, 'seq', axis=1, tiled=True)]
    all_gather x2 -> x0, local copies, waits for them, and re-layouts: 6.89 us -> none  [the longest x1 3.97 us: local(): lax.all_gather(cached_prompt_values[0], ('pair', 'seq'), axis=0, tiled=True)]
    unnamed x7 -> x0, local copies, waits for them, and re-layouts: 4 us -> none
  transfers between devices with their start and end apart: 4 -> 0, of which waited for: 4 -> 0; matrix products, arithmetic and copies ran while one was open for 7% -> 0% of each run, Pallas kernels for 0% -> 0%
where the time goes in v1:
time: 81.2 us; the launch traced here: 81.1 us
  Pallas kernels  77.7 us (96%)
  other arithmetic  2.05 us (3%)
  between operations  1.31 us (2%)
    pallas_call x1, Pallas kernels, attention(): pl.pallas_call(kernel, out_shape=jax.ShapeDtypeStruct((ROWS, KV_HEADS * G...  77.7 us
    broadcast_in_dim x1, other arithmetic, local(): return jnp.where(live, mixed, jnp.zeros((), BF16))[None, None]  2.04 us

profile of v1, /device:TPU:1, one launch (start us, length us, event | category | flops | bytes accessed | tf_op | source)
XLA Modules:
  0.0 81.1 jit_solution(17599570070341623640)
XLA Ops:
  1.3 77.7 %shard_map.82 = bf16[128,2560]{1,0:T(8,128)(2,1)} custom-call(bf16[1,1,128,5120]{3,2,1,0:T(8,128)(2,1)} %x_ref.1, bf16[1,1,128,2560]{3,2,1,0:T(8,128)(2,1)} %q_ref.1, bf16[320,512]{1,0:T(8,128)(2,1)} %kw_ref.1, bf16[320,512]{1,0:T(8,128)(2,1)} %vw_ref.1, bf16[1,64,512]{2,1,0:T(8,128)(2,1)} %pk_ref.1, bf16[1,64,512]{2,1,0:T(8,128)(2,1)} %pv_ref.1, ...), custom_call_target="tpu_custom_call" | custom-call | flops 4400000000 | bytes 8000000 | tf_op jit(solution)/shard_map/pallas_call | solution.py:391
  79.0 2.0 %select_bitcast_fusion = bf16[1,1,128,2560]{3,2,1,0:T(8,128)(2,1)} fusion(bf16[128,2560]{1,0:T(8,128)(2,1)} %shard_map.82, pred[128]{0:T(512)(128)(4,1)S(1)} %add_compare_fusion), kind=kLoop, calls=%fused_computation | loop fusion | flops 327680 | bytes 1310848 | tf_op jit(solution)/shard_map/broadcast_in_dim | solution.py:432
  (1 shorter events, 0.0 us)

commit v2 on v0

v2 whole, which is shorter than its diff:
```python
import functools
import math

import jax
import jax.numpy as jnp
from jax import lax
from jax.experimental import pallas as pl
from jax.experimental.pallas import tpu as pltpu
from jax.sharding import PartitionSpec as P

KV_HEADS = 4
HEAD = 128
GROUP = 5
NY, NZ, NX = 8, 8, 4
ROWS = 128
SHARD = 64
BLOCK = NX * SHARD
WROWS = 320
XCOLS = 2 * WROWS
WCOLS = HEAD
QROWS = GROUP * ROWS
NEG = -1e30
SCALE = HEAD ** (-0.5) * math.log2(math.e)
MESH = pl.DeviceIdType.MESH
F32 = jnp.float32
BF16 = jnp.bfloat16
LIMIT = dict(z=6, y=5, hx=4, sx=3, sib=8)
HOP = 5.5
WAVES = (0.0, 0.3, 0.6, 0.9)
XTIME = (0.0, 3.5, 4.5, 7.0)
ZTIME = (6.5, 10.5, 11.5, 14.0)
ZHOP = (5.0, 6.5, 6.5, 6.5)
REACH = ((4, 3), (3, 4))
WAVE_HEADS = (1, 2, 0, 3)


def kernel(
    x_ref, q_ref, kw_ref, vw_ref, pk_ref, pv_ref, plen_ref, o_ref,
    kvbuf, wbuf, xin, xsend, xbuf, qs, pacc, psend, precv, newkv, top_ref, den_ref, acc_ref,
    own_sem, q_sem, xl_sem, wl_sem,
    ph_s, ph_r, zs_s, zs_r, zt_s, zt_r, h_s, h_r, y_s, y_r, b_s, b_r, x_s, x_r, p_s, p_r,
):
    blk, pair, s = lax.axis_index("blk"), lax.axis_index("pair"), lax.axis_index("seq")
    y, c = blk // 2, blk % 2
    z, hi = pair // 2, pair % 2
    x = hi * 2 + s
    up = 1 - 2 * (y % 2)
    heads = (1, 2, 3 * s, 3 * (1 - s))
    lanes = tuple(pl.ds(pl.multiple_of(h * HEAD, HEAD), HEAD) for h in heads)

    def y_dev(step):
        return {"blk": ((y + step + NY) % NY) * 2 + c, "pair": pair, "seq": s}

    def z_dev(step):
        return {"blk": blk, "pair": ((z + step + NZ) % NZ) * 2 + hi, "seq": s}

    sib = {"blk": y * 2 + (1 - c), "pair": pair, "seq": s}
    sx = {"blk": blk, "pair": pair, "seq": 1 - s}
    hx = {"blk": blk, "pair": z * 2 + (1 - hi), "seq": 1 - s}
    x2 = {"blk": blk, "pair": z * 2 + (1 - hi), "seq": s}
    x_peers = (sx, hx, x2)

    def slot(p):
        return pl.ds((p + 1) * SHARD, SHARD)

    def remote(src, dst, ss, rs, dev):
        return pltpu.make_async_remote_copy(
            src_ref=src, dst_ref=dst, send_sem=ss, recv_sem=rs, device_id=dev, device_id_type=MESH
        )

    flying = {}

    def go(link, copy, start=True):
        queue = flying.setdefault(link, [])
        if len(queue) >= LIMIT[link[0]]:
            queue.pop(0).wait_send()
        if start:
            copy.start()
        queue.append(copy)


    local_q = [
        pltpu.make_async_copy(
            q_ref.at[0, 0, :, pl.ds(pl.multiple_of((heads[n] * GROUP + g) * HEAD, HEAD), HEAD)],
            qs.at[n, pl.ds(g * ROWS, ROWS)],
            q_sem.at[n * GROUP + g],
        )
        for n in range(KV_HEADS)
        for g in range(GROUP)
    ]
    cached = (pk_ref, pv_ref)
    own_rows = pl.ds(0, SHARD)
    local_kv = [
        pltpu.make_async_copy(cached[i].at[0], kvbuf.at[i, z, own_rows], own_sem.at[i]) for i in range(2)
    ]
    own_x_rows = pl.ds(pl.multiple_of(s * ROWS, ROWS), ROWS)
    local_x = pltpu.make_async_copy(x_ref.at[0, 0], xin, xl_sem.at[0])
    weights = (kw_ref, vw_ref)

    def w_cols(g):
        return weights[g // KV_HEADS].at[:, pl.ds((g % KV_HEADS) * WCOLS, WCOLS)]

    def w_ref(g, yy):
        kv, n = g if isinstance(g, tuple) else divmod(g, KV_HEADS)
        rows = pl.ds(pl.multiple_of((yy % 2) * WROWS, 64), WROWS)
        return wbuf.at[kv, yy // 2, rows, pl.ds(n * WCOLS, WCOLS)]

    owner = c * 2 + s

    def local_w(g):
        return pltpu.make_async_copy(w_cols(g), w_ref(g, y), wl_sem.at[g])

    local_x.start()
    for copy in local_kv + local_q:
        copy.start()

    @pl.when(c == s)
    def _():
        for g in range(2 * KV_HEADS):
            local_w(g).start()

    barrier = pltpu.get_barrier_semaphore()
    for dev in (sib, sx, hx, x2, y_dev(1), y_dev(-1), z_dev(1), z_dev(-1)):
        pl.semaphore_signal(barrier, inc=1, device_id=dev, device_id_type=MESH)
    pl.semaphore_wait(barrier, 8)

    phase = []
    for p in (0, 1, 2):
        for i in range(2):
            copy = remote(cached[i].at[0], kvbuf.at[i, z, slot(p)], ph_s.at[i, p], ph_r.at[i, p], x_peers[p])
            copy.start()
            phase.append((i, p, copy))

    def y_from(way, d):
        return (y - d + NY) % NY if way == 0 else (y + d) % NY

    def y_send(way, n, d, src=None):
        ref = w_ref((c, n), y_from(way, d))
        return remote(
            ref if src is None else src, ref, y_s.at[way, n, d], y_r.at[way, n, d + 1], y_dev(1 - 2 * way)
        )

    def y_recv(way, n, d):
        ref = w_ref((c, n), y_from(way, d))
        return remote(ref, ref, y_s.at[way, n, d], y_r.at[way, n, d], y_dev(2 * way - 1))

    def sib_copy(g, yy, src=None):
        ref = w_ref(g, yy)
        kv, n = g if isinstance(g, tuple) else divmod(g, KV_HEADS)
        return remote(ref if src is None else src, ref, b_s.at[kv, n, yy], b_r.at[kv, n, yy], sib)

    def y_start(n):
        for way in range(2):
            go(("y", way), y_send(way, n, 0), start=False)
        for cc in range(2):

            @pl.when(owner == 3 * cc)
            def _():
                for way in range(2):
                    y_send(way, n, 0, w_cols(KV_HEADS * cc + n)).start()

            @pl.when(owner == 2 - cc)
            def _():
                sib_copy((c, n), y).wait_recv()
                for way in range(2):
                    y_send(way, n, 0).start()

    for cc in range(2):

        @pl.when(owner == 3 * cc)
        def _():
            for kv in (1 - cc, cc):
                for n in WAVE_HEADS:
                    sib_copy(KV_HEADS * kv + n, y, w_cols(KV_HEADS * kv + n)).start()

    def y_event(way, n, d):
        y_recv(way, n, d).wait_recv()
        if d < REACH[way][n % 2]:
            go(("y", way), y_send(way, n, d))
        go(("sib",), sib_copy((c, n), y_from(way, d)))

    ring_cols = pl.ds(pl.multiple_of(s * HEAD, HEAD), 3 * HEAD)
    give_cols = pl.ds(pl.multiple_of(s * 3 * HEAD, HEAD), HEAD)
    take_cols = pl.ds(pl.multiple_of((1 - s) * 3 * HEAD, HEAD), HEAD)

    def z_from(way, d):
        return (z - d + NZ) % NZ if way == 0 else (z + d) % NZ

    def z_reach(way, i):
        return REACH[way][i]

    def z_ref(stream, way, i, d):
        return kvbuf.at[i, z_from(way, d), pl.ds(stream * SHARD, SHARD), ring_cols]

    def z_send(stream, way, i, d, src=None):
        ref = z_ref(stream, way, i, d)
        return remote(
            ref if src is None else src, ref, zs_s.at[stream, way, i, d], zs_r.at[stream, way, i, d + 1],
            z_dev(1 - 2 * way),
        )

    def z_recv(stream, way, i, d):
        ref = z_ref(stream, way, i, d)
        return remote(ref, ref, zs_s.at[stream, way, i, d], zs_r.at[stream, way, i, d], z_dev(2 * way - 1))

    def h_send(way, i, d):
        ref = kvbuf.at[i, z_from(way, d), :, give_cols]
        return remote(ref, ref, h_s.at[way, i, d], h_r.at[way, i, d], hx)

    def h_recv(way, i, d):
        ref = kvbuf.at[i, z_from(way, d), :, take_cols]
        return remote(ref, ref, h_s.at[way, i, d], h_r.at[way, i, d], hx)

    def z_event(stream, way, i, d):
        z_recv(stream, way, i, d).wait_recv()
        if d < z_reach(way, i):
            go(("z", way), z_send(stream, way, i, d))
        if stream == NX - 1 and d < 4:
            go(("hx",), h_send(way, i, d))

    def take_send(i, d):
        ref = kvbuf.at[i, z_from(i, d), :, take_cols]
        return remote(ref, ref, zt_s.at[i], zt_r.at[i], z_dev(1 - 2 * i))

    def take_event(i):
        h_recv(i, i, 3).wait_recv()
        go(("z", i), take_send(i, 3))

    order = (y, (y - up + NY) % NY, (y + 2 * up + NY) % NY, (y + 4) % NY)

    def x_part(t, parity):
        first = 2 * t * XCOLS + parity * WROWS
        return jnp.concatenate(
            [xin[:, first : first + WROWS], xin[:, first + XCOLS : first + XCOLS + WROWS]], axis=1
        )

    def split_x():
        local_x.wait()
        for parity in range(2):

            @pl.when(s == parity)
            def _():
                for t in range(4):
                    xsend[t] = x_part(t, 1 - parity)
                    xbuf[t, parity * ROWS : (parity + 1) * ROWS] = x_part(t, parity)

    def send_x(first, last):
        for yy in order[first:last]:
            t = yy // 2
            go(("sx",), remote(xsend.at[t], xbuf.at[t, own_x_rows], x_s.at[t], x_r.at[t], sx))

    other_x_rows = pl.ds(pl.multiple_of((1 - s) * ROWS, ROWS), ROWS)

    def z_start(stream, i):
        if stream > 0:
            ref = kvbuf.at[i, z, slot(stream - 1)]
            remote(ref, ref, ph_s.at[i, stream - 1], ph_r.at[i, stream - 1], x_peers[stream - 1]).wait_recv()
        for way in range(2):
            go(("z", way), z_send(stream, way, i, 0, cached[i].at[0, :, ring_cols] if stream == 0 else None))

    live_prompt = plen_ref[0]

    def update(h, score, value, first):
        best = functools.reduce(jnp.maximum, [jnp.max(v, axis=1, keepdims=True) for v in score])
        if first:
            top = jnp.broadcast_to(best, (QROWS, HEAD))
        else:
            old = top_ref[h]
            top = jnp.maximum(old, best)
            fade = jnp.exp2(old - top)
        weight = [jnp.exp2(v - top[:, :1]) for v in score]
        den = functools.reduce(
            jnp.add,
            [w[:, j * HEAD : (j + 1) * HEAD] for w in weight for j in range(w.shape[1] // HEAD)],
        )
        out = functools.reduce(
            jnp.add,
            [jnp.dot(w.astype(BF16), v, preferred_element_type=F32) for w, v in zip(weight, value)],
        )
        if not first:
            den = den + den_ref[h] * fade
            out = out + acc_ref[h] * fade
        return top, den, out

    def dot_t(a, b):
        return lax.dot_general(a, b, (((1,), (1,)), ((), ())), preferred_element_type=F32)

    def prompt_piece(n, d, zb):
        away = int(d > 0 and n == KV_HEADS - 1)
        ehi, es = (1 - hi, 1 - s) if away else (hi, s)
        col = lax.broadcasted_iota(jnp.int32, (1, BLOCK), 1)
        shard = jnp.where(
            col < SHARD,
            ehi * 2 + es,
            jnp.where(
                col < 2 * SHARD,
                ehi * 2 + 1 - es,
                jnp.where(col < 3 * SHARD, (1 - ehi) * 2 + 1 - es, (1 - ehi) * 2 + es),
            ),
        )
        pos = zb * BLOCK + shard * SHARD + col % SHARD
        shut = jnp.where(pos < live_prompt, 0.0, NEG)
        return dot_t(qs[n], kvbuf[0, zb, :, lanes[n]]) * SCALE + shut, kvbuf[1, zb, :, lanes[n]]

    def attend(h, d):
        blocks = [z] if d == 0 else [z_from(way, d) for way in range(2)]
        score, value = zip(*(prompt_piece(h, d, zb) for zb in blocks))
        top, den, out = update(h, score, value, d == 0)
        top_ref[h] = top
        den_ref[h] = den
        acc_ref[h] = out

    def wait_own():
        for copy in local_q + local_kv:
            copy.wait()

    def wait_neighbour(d):
        for way in range(2):
            for i in range(2):
                if d == 4 and way == 0:
                    take_send(i, 4).wait_recv()
                if d < 3 or (d == 3 and way != i):
                    h_recv(way, i, d).wait_recv()

    def project(m, p):
        kv = c if m == 0 else 1 - c
        t = order[p] // 2
        if p == 0:

            @pl.when(c == s)
            def _():
                for n in range(KV_HEADS):
                    pltpu.make_async_copy(w_cols(n), w_ref((kv, n), y), wl_sem.at[kv * KV_HEADS + n]).wait()

            if m == 1:

                @pl.when(c != s)
                def _():
                    for n in range(KV_HEADS):
                        sib_copy((kv, n), y).wait_recv()

        if m == 1:
            for n in range(KV_HEADS):
                if p > 0:
                    sib_copy((kv, n), order[p]).wait_recv()
                sib_copy((kv, n), 4 * t + 1 - order[p]).wait_recv()
        if m == 0:
            ref = xbuf.at[t, other_x_rows]
            remote(ref, ref, x_s.at[t], x_r.at[t], sx).wait_recv()
        if p < 3:
            add = jnp.dot(xbuf[t], wbuf[kv, t], preferred_element_type=F32)
            pacc[kv] = add if p == 0 else pacc[kv] + add
        else:
            for half in range(2):
                cols = slice(half * 2 * HEAD, (half + 1) * 2 * HEAD)
                total = pacc[kv, :, cols] + jnp.dot(xbuf[t], wbuf[kv, t, :, cols], preferred_element_type=F32)
                pacc[kv, :, cols] = total
                psend[kv, half] = total.astype(BF16)
                go(("sx",), part_copy(kv, half))

    def part_copy(kv, half):
        return remote(psend.at[kv, half], precv.at[kv, half], p_s.at[kv, half], p_r.at[kv, half], sx)

    def join(half):
        cols = slice(half * 2 * HEAD, (half + 1) * 2 * HEAD)
        for kv in range(2):
            part_copy(kv, half).wait_recv()
            newkv[kv, :, cols] = (pacc[kv, :, cols] + precv[kv, half].astype(F32)).astype(BF16)

    def finish(n):
        row = lax.broadcasted_iota(jnp.int32, (QROWS, 2 * ROWS), 0) % ROWS + s * ROWS
        col = lax.broadcasted_iota(jnp.int32, (QROWS, 2 * ROWS), 1)
        shut = jnp.where(col <= row, 0.0, NEG)
        score, value = prompt_piece(n, 4, z_from(0, 4))
        new_score = dot_t(qs[n], newkv[0, :, lanes[n]]) * SCALE + shut
        _, den, out = update(n, [score, new_score], [value, newkv[1, :, lanes[n]]], False)
        out = out / jnp.sum(den, axis=1, keepdims=True)
        for g in range(GROUP):
            cols = pl.ds(pl.multiple_of((heads[n] * GROUP + g) * HEAD, HEAD), HEAD)
            o_ref[:, cols] = out[g * ROWS : (g + 1) * ROWS].astype(BF16)

    events, tasks = [], []

    def event(time, fn, *args):
        events.append((time, len(events), fn, args))

    def task(time, length, fn, *args):
        tasks.append((time, length, fn, args))

    for stream in range(NX):
        for i in range(2):
            event(XTIME[stream] + 0.5 * i, z_start, stream, i)
            for way in range(2):
                for d in range(1, z_reach(way, i) + 1):
                    event(ZTIME[stream] + ZHOP[stream] * (d - 1) + 0.5 * i, z_event, stream, way, i, d)
    event(0.6, split_x)
    event(XTIME[2] + 0.6, send_x, 0, 1)
    event(XTIME[3] + 0.6, send_x, 1, 4)
    full = [ZTIME[3] + ZHOP[3] * (d - 1) + 0.6 for d in range(5)]
    event(full[3] + 3.5, take_event, 0)
    event(full[3] + 4.0, take_event, 1)
    for wave, n in zip(WAVES, WAVE_HEADS):
        event(wave + 2.0, y_start, n)
        for way in range(2):
            for d in range(1, REACH[way][n % 2] + 1):
                event(wave + 2.5 + HOP * d, y_event, way, n, d)
    for p in range(4):
        for m in range(2):
            ready = max(11.0 + 3.5 * p, WAVES[3] + 2.6 + HOP * (p + 1) + 2.5 * m)
            task(ready, 0.7, project, m, p)
    for half in range(2):
        task(ready + 6.0 + 2.0 * half, 0.5, join, half)
    task(9.0, 0.0, wait_own)
    for d in range(4):
        ready = 9.0 if d == 0 else full[d]
        for n in range(KV_HEADS):
            if d and n == KV_HEADS - 1:
                ready += 4.1
                task(ready, 0.0, wait_neighbour, d)
            task(ready, 0.7 if d else 0.4, attend, n, d)
    tasks.sort(key=lambda e: (e[2] not in (project, join), e[0]))
    events.sort(key=lambda e: e[:2])
    now = 0.0
    while events or tasks:
        ready = [t for t in tasks if t[0] <= now]
        if events and events[0][0] <= now:
            _, _, fn, args = events.pop(0)
            fn(*args)
            now += 0.1
        elif ready:
            tasks.remove(ready[0])
            _, length, fn, args = ready[0]
            fn(*args)
            now += length
        else:
            now = min([e[0] for e in events[:1]] + [t[0] for t in tasks])
    for n in range(KV_HEADS):
        if n == KV_HEADS - 1:
            wait_neighbour(4)
        finish(n)

    for queue in flying.values():
        for copy in queue:
            copy.wait_send()
    for _, _, copy in phase:
        copy.wait_send()

    @pl.when(c == s)
    def _():
        for g in range(2 * KV_HEADS):
            sib_copy(g, y).wait_send()


def attention(resp_x, queries, key_weight, value_weight, prompt_key, prompt_values, prompt_len):
    dma = pltpu.SemaphoreType.DMA
    any_space = pl.BlockSpec(memory_space=pl.ANY)
    return pl.pallas_call(
        kernel,
        out_shape=jax.ShapeDtypeStruct((ROWS, KV_HEADS * GROUP * HEAD), BF16),
        in_specs=[any_space] * 6 + [pl.BlockSpec(memory_space=pltpu.SMEM)],
        out_specs=pl.BlockSpec(memory_space=pltpu.VMEM),
        scratch_shapes=[
            pltpu.VMEM((2, NZ, BLOCK, KV_HEADS * HEAD), BF16),
            pltpu.VMEM((2, 4, XCOLS, 4 * WCOLS), BF16),
            pltpu.VMEM((ROWS, 8 * XCOLS), BF16),
            pltpu.VMEM((4, ROWS, XCOLS), BF16),
            pltpu.VMEM((4, 2 * ROWS, XCOLS), BF16),
            pltpu.VMEM((KV_HEADS, QROWS, HEAD), BF16),
            pltpu.VMEM((2, 2 * ROWS, 4 * WCOLS), F32),
            pltpu.VMEM((2, 2, 2 * ROWS, 2 * WCOLS), BF16),
            pltpu.VMEM((2, 2, 2 * ROWS, 2 * WCOLS), BF16),
            pltpu.VMEM((2, 2 * ROWS, 4 * WCOLS), BF16),
            pltpu.VMEM((KV_HEADS, QROWS, HEAD), F32),
            pltpu.VMEM((KV_HEADS, QROWS, HEAD), F32),
            pltpu.VMEM((KV_HEADS, QROWS, HEAD), F32),
            dma((2,)), dma((KV_HEADS * GROUP,)), dma((1,)), dma((8,)),
            dma((2, 3)), dma((2, 3)),
            dma((4, 2, 2, 5)), dma((4, 2, 2, 5)),
            dma((2,)), dma((2,)),
            dma((2, 2, 5)), dma((2, 2, 5)),
            dma((2, 4, 5)), dma((2, 4, 5)),
            dma((2, 4, 8)), dma((2, 4, 8)),
            dma((4,)), dma((4,)),
            dma((2, 2)), dma((2, 2)),
        ],
        compiler_params=pltpu.CompilerParams(
            collective_id=0, has_side_effects=True, vmem_limit_bytes=56 << 20
        ),
        cost_estimate=pl.CostEstimate(flops=4_400_000_000, bytes_accessed=8_000_000, transcendentals=6_000_000),
    )(resp_x, queries, key_weight, value_weight, prompt_key, prompt_values, prompt_len)


def local(
    resp_x, queries, key_weight, value_weight, prompt_key, cached_prompt_values, lengths, prompt_len
):
    mixed = attention(
        resp_x, queries, key_weight, value_weight, prompt_key, cached_prompt_values, prompt_len
    )
    row = lax.axis_index("seq") * ROWS + jnp.arange(ROWS, dtype=jnp.int32)
    live = (row < lengths[0, 0])[:, None]
    return jnp.where(live, mixed, jnp.zeros((), BF16))[None, None]


def solution(mesh):
    return jax.shard_map(
        local,
        mesh=mesh,
        in_specs=(
            P("blk", "pair", "seq", None),
            P("blk", "pair", "seq", None),
            P("blk", None),
            P("blk", None),
            P("blk", ("pair", "seq"), None),
            P("blk", ("pair", "seq"), None),
            P("blk", "pair"),
            P("blk"),
        ),
        out_specs=P("blk", "pair", "seq", None),
        check_vma=False,
    )
```

time: 321 us -> 67.1 us (0.21)
  the two profiles are of different devices: /device:TPU:1 before, /device:TPU:2 now
where the time goes in v2:
time: 67.1 us; the launch traced here: 66.9 us
  Pallas kernels  63.6 us (95%)
  other arithmetic  2.05 us (3%)
  between operations  1.31 us (2%)
    pallas_call x1, Pallas kernels, attention(): pl.pallas_call(kernel, out_shape=jax.ShapeDtypeStruct((ROWS, KV_HEADS * G...  63.6 us
    broadcast_in_dim x1, other arithmetic, local(): return jnp.where(live, mixed, jnp.zeros((), BF16))[None, None]  2.04 us

profile of v2, /device:TPU:2, one launch (start us, length us, event | category | flops | bytes accessed | tf_op | source)
XLA Modules:
  0.0 66.9 jit_solution(8708714970007596431)
XLA Ops:
  1.3 63.6 %shard_map.82 = bf16[128,2560]{1,0:T(8,128)(2,1)} custom-call(bf16[1,1,128,5120]{3,2,1,0:T(8,128)(2,1)} %x_ref.1, bf16[1,1,128,2560]{3,2,1,0:T(8,128)(2,1)} %q_ref.1, bf16[320,512]{1,0:T(8,128)(2,1)} %kw_ref.1, bf16[320,512]{1,0:T(8,128)(2,1)} %vw_ref.1, bf16[1,64,512]{2,1,0:T(8,128)(2,1)} %pk_ref.1, bf16[1,64,512]{2,1,0:T(8,128)(2,1)} %pv_ref.1, ...), custom_call_target="tpu_custom_call" | custom-call | flops 4400000000 | bytes 8000000 | tf_op jit(solution)/shard_map/pallas_call | solution.py:457
  64.9 2.0 %select_bitcast_fusion = bf16[1,1,128,2560]{3,2,1,0:T(8,128)(2,1)} fusion(bf16[128,2560]{1,0:T(8,128)(2,1)} %shard_map.82, pred[128]{0:T(512)(128)(4,1)S(1)} %add_compare_fusion), kind=kLoop, calls=%fused_computation | loop fusion | flops 327680 | bytes 1310848 | tf_op jit(solution)/shard_map/broadcast_in_dim | solution.py:501
  (1 shorter events, 0.0 us)

commit v3 on v2

--- a/solution.py
+++ b/solution.py
@@ -397,8 +397,8 @@
     event(XTIME[2] + 0.6, send_x, 0, 1)
     event(XTIME[3] + 0.6, send_x, 1, 4)
     full = [ZTIME[3] + ZHOP[3] * (d - 1) + 0.6 for d in range(5)]
-    event(full[3] + 3.5, take_event, 0)
-    event(full[3] + 4.0, take_event, 1)
+    event(full[3] + 2.0, take_event, 0)
+    event(full[3] + 2.5, take_event, 1)
     for wave, n in zip(WAVES, WAVE_HEADS):
         event(wave + 2.0, y_start, n)
         for way in range(2):
@@ -408,14 +408,13 @@
         for m in range(2):
             ready = max(11.0 + 3.5 * p, WAVES[3] + 2.6 + HOP * (p + 1) + 2.5 * m)
             task(ready, 0.7, project, m, p)
-    for half in range(2):
-        task(ready + 6.0 + 2.0 * half, 0.5, join, half)
+    task(ready + 6.0, 0.5, join, 0)
     task(9.0, 0.0, wait_own)
     for d in range(4):
         ready = 9.0 if d == 0 else full[d]
         for n in range(KV_HEADS):
             if d and n == KV_HEADS - 1:
-                ready += 4.1
+                ready += 2.6
                 task(ready, 0.0, wait_neighbour, d)
             task(ready, 0.7 if d else 0.4, attend, n, d)
     tasks.sort(key=lambda e: (e[2] not in (project, join), e[0]))
@@ -435,6 +434,8 @@
         else:
             now = min([e[0] for e in events[:1]] + [t[0] for t in tasks])
     for n in range(KV_HEADS):
+        if n == 1:
+            join(1)
         if n == KV_HEADS - 1:
             wait_neighbour(4)
         finish(n)

time: 67.1 us -> 65.8 us (0.981)
  the two profiles are of different devices: /device:TPU:2 before, /device:TPU:24 now
where the time goes in v3:
time: 65.8 us; the launch traced here: 65.6 us
  Pallas kernels  62.3 us (95%)
  other arithmetic  2.05 us (3%)
  between operations  1.31 us (2%)
    pallas_call x1, Pallas kernels, attention(): pl.pallas_call(kernel, out_shape=jax.ShapeDtypeStruct((ROWS, KV_HEADS * G...  62.3 us
    broadcast_in_dim x1, other arithmetic, local(): return jnp.where(live, mixed, jnp.zeros((), BF16))[None, None]  2.04 us

profile of v3, /device:TPU:24, one launch (start us, length us, event | category | flops | bytes accessed | tf_op | source)
XLA Modules:
  0.0 65.6 jit_solution(16573660156510518494)
XLA Ops:
  1.3 62.3 %shard_map.82 = bf16[128,2560]{1,0:T(8,128)(2,1)} custom-call(bf16[1,1,128,5120]{3,2,1,0:T(8,128)(2,1)} %x_ref.1, bf16[1,1,128,2560]{3,2,1,0:T(8,128)(2,1)} %q_ref.1, bf16[320,512]{1,0:T(8,128)(2,1)} %kw_ref.1, bf16[320,512]{1,0:T(8,128)(2,1)} %vw_ref.1, bf16[1,64,512]{2,1,0:T(8,128)(2,1)} %pk_ref.1, bf16[1,64,512]{2,1,0:T(8,128)(2,1)} %pv_ref.1, ...), custom_call_target="tpu_custom_call" | custom-call | flops 4400000000 | bytes 8000000 | tf_op jit(solution)/shard_map/pallas_call | solution.py:458
  63.6 2.0 %select_bitcast_fusion = bf16[1,1,128,2560]{3,2,1,0:T(8,128)(2,1)} fusion(bf16[128,2560]{1,0:T(8,128)(2,1)} %shard_map.82, pred[128]{0:T(512)(128)(4,1)S(1)} %add_compare_fusion), kind=kLoop, calls=%fused_computation | loop fusion | flops 327680 | bytes 1310848 | tf_op jit(solution)/shard_map/broadcast_in_dim | solution.py:502
  (1 shorter events, 0.0 us)
